TPU v7x, 512 devices: a whole 4x8x8 slice. The times are simulated.
512 devices in a mesh: heads: 8 (over z_lo, core), tm: 64 (over x, y, z_hi).
Axes of the slice: x: 4, y: 8, z: 8 (z_hi: 2, z_lo: 4; z = z_hi * 4 + z_lo), core: 2. Of those that a mesh axis runs over, the one named last changes fastest.
Arguments:
- queries: bfloat16 [16384, 3072], P('tm', 'heads'), parts along dimension 1, may hold values from -8 to 8
- keys: bfloat16 [16384, 3072], P('tm', 'heads'), parts along dimension 1, may hold values from -8 to 8
- values: bfloat16 [16384, 3072], P('tm', 'heads'), parts along dimension 1, may hold values from -6 to 6
- positions: int32 [3, 16384], P(None, 'tm'), may hold values from 0 to 79, as said below
- tile_masks: int32 [128, 8, 2], P('tm'), may hold values from 0 to 1, as said below
- sink_index: int32 [256], replicated, may hold values from 0 to 3599, as said below
Outputs:
- attended: bfloat16 [16384, 3072], P('tm', 'heads'), parts along dimension 1
There are 8 independent parts, one for each index of `heads`. A program takes and returns all parts, laid end to end along the dimension named above; an argument that names none is the same for every part. Nothing has to cross between parts.
Inputs may be any that keep to these rules, and one draw needn't show every extreme that they name: `positions`: consecutive tokens of the latent video of 33 x 45 x 80, row by row, from some starting token. `tile_masks`: tiles of farther partners are kept less often. `sink_index`: distinct rows among the first min(16384, 3600) of the window.
All inputs are finite; a program needn't handle non-finite values.
Results may differ from a plain program's by a relative error of at most 0.0085.
The roundings to bfloat16 on the way count: a program that leaves them out, or rounds other values in their place, can miss the bound.
Values may be sent and summed in bfloat16 or wider, within the bound.
A program may use at most 64 MiB of HBM per device.

v0:
```python
import jax
import jax.numpy as jnp
from jax import lax
from jax.sharding import PartitionSpec as P

HG = 3
HD = 128
TILE = 128
NOFF = 4
SINK = 256


def shifted(shard, axis, by):
    length = lax.axis_size(axis)
    pairs = [(i, i + by) for i in range(length) if 0 <= i + by < length]
    return lax.ppermute(shard, axis, pairs)


def rotate(row_data, position, factor):
    row_count = row_data.shape[0]
    first_size = HD // 8
    second_size = (HD - HD // 8) // 2
    section_sizes = (first_size, second_size, HD - first_size - second_size)
    angle_list = []
    for axis_id in range(3):
        section_width = section_sizes[axis_id]
        inverse = 256.0 ** (-jnp.arange(0, section_width, 2).astype(jnp.float32) / section_width)
        angle_list.append(position[axis_id].astype(jnp.float32)[:, None] * inverse[None, :])
    angle_all = jnp.concatenate(angle_list, axis=1)
    cosine = jnp.cos(angle_all)[:, None, :]
    sine_part = jnp.sin(angle_all)[:, None, :]
    pair_view = row_data.astype(jnp.float32).reshape(row_count, HG, HD // 2, 2)
    even_part = pair_view[..., 0]
    odd_part = pair_view[..., 1]
    turned = jnp.stack(
        [even_part * cosine - odd_part * sine_part, even_part * sine_part + odd_part * cosine],
        axis=-1,
    )
    return (turned * factor).reshape(row_count, HG * HD)


def block_part(query_heads, key_heads, value_heads, tile_keep):
    keep_mask = jnp.repeat(jnp.repeat(tile_keep, TILE, axis=0), TILE, axis=1)[:, None, :]
    scores = jnp.einsum("qhd,khd->qhk", query_heads, key_heads, preferred_element_type=jnp.float32)
    masked = jnp.where(keep_mask > 0, scores, -1e30)
    row_max = jnp.max(masked, axis=2)
    weights = jnp.exp(masked - row_max[:, :, None]) * keep_mask
    totals = jnp.sum(weights, axis=2)
    weighted = jnp.einsum(
        "qhk,khd->qhd",
        weights.astype(jnp.bfloat16),
        value_heads,
        preferred_element_type=jnp.float32,
    )
    return (weighted, row_max, totals)


def combine_parts(first, second):
    weighted_a, max_a, total_a = first
    weighted_b, max_b, total_b = second
    new_max = jnp.maximum(max_a, max_b)
    scale_first = jnp.exp(max_a - new_max)
    scale_second = jnp.exp(max_b - new_max)
    weighted = weighted_a * scale_first[:, :, None] + weighted_b * scale_second[:, :, None]
    return (weighted, new_max, total_a * scale_first + total_b * scale_second)


def on_device(queries, keys, values, positions, tile_masks, sink_index):
    rows_here = queries.shape[0]
    shards = lax.axis_size("tm")
    index_here = lax.axis_index("tm")
    feature_width = HG * HD
    tiles = rows_here // TILE
    q_rot = rotate(queries, positions, HD ** (-0.5)).astype(jnp.bfloat16)
    k_rot = rotate(keys, positions, 1.0).astype(jnp.bfloat16)
    query_heads = q_rot.reshape(rows_here, HG, HD)
    key_heads = k_rot.reshape(rows_here, HG, HD)
    value_heads = values.reshape(rows_here, HG, HD)
    state = block_part(query_heads, key_heads, value_heads, jnp.ones((tiles, tiles), jnp.float32))
    local_index = sink_index - index_here * rows_here
    one_hot = (local_index[:, None] == jnp.arange(rows_here, dtype=jnp.int32)[None, :]).astype(
        jnp.bfloat16
    )
    sink_table = jnp.dot(
        one_hot, jnp.concatenate([k_rot, values], axis=1), preferred_element_type=jnp.float32
    )
    sink_table = lax.psum(sink_table, "tm").astype(jnp.bfloat16)
    sink_keys = sink_table[:, :feature_width].reshape(SINK, HG, HD)
    sink_values = sink_table[:, feature_width:].reshape(SINK, HG, HD)
    sink_keep = jnp.ones((tiles, SINK // TILE), jnp.float32)
    state = combine_parts(state, block_part(query_heads, sink_keys, sink_values, sink_keep))
    mask_float = tile_masks.astype(jnp.float32)
    for offset in range(1, NOFF + 1):
        reverse_mask = tile_masks[:, NOFF + offset - 1, :].astype(jnp.bfloat16)
        their_queries, their_keys, their_values, their_mask = shifted(
            (q_rot, k_rot, values, reverse_mask), "tm", -offset
        )
        later_ok = (index_here + offset < shards).astype(jnp.float32)
        earlier_ok = (index_here - offset >= 0).astype(jnp.float32)
        mine_part = block_part(
            query_heads,
            their_keys.reshape(rows_here, HG, HD),
            their_values.reshape(rows_here, HG, HD),
            mask_float[:, offset - 1, :] * later_ok,
        )
        state = combine_parts(state, mine_part)
        returned = block_part(
            their_queries.reshape(rows_here, HG, HD),
            key_heads,
            value_heads,
            their_mask.astype(jnp.float32),
        )
        back_weighted, back_max, back_totals = shifted(
            (returned[0], returned[1], returned[2]), "tm", offset
        )
        back_max = jnp.where(earlier_ok > 0, back_max, -1e30)
        state = combine_parts(
            state, (back_weighted * earlier_ok, back_max, back_totals * earlier_ok)
        )
    weighted, row_max, totals = state
    return (weighted / totals[:, :, None]).astype(jnp.bfloat16).reshape(rows_here, feature_width)


def solution(mesh):
    in_specs = (
        P("tm", "heads"),
        P("tm", "heads"),
        P("tm", "heads"),
        P(None, "tm"),
        P("tm", None, None),
        P(),
    )
    out_specs = P("tm", "heads")
    return jax.shard_map(
        on_device, mesh=mesh, in_specs=in_specs, out_specs=out_specs, check_vma=False
    )
```

profile of v0, /device:TPU:4, one launch (start us, length us, event | category | flops | bytes accessed | tf_op | source)
XLA Modules:
  0.0 699.2 jit_solution(151011124536786140)
XLA Ops:
  0.0 13.8 %collective-permute-start.1 = (bf16[256,384]{1,0:T(8,128)(2,1)}, bf16[256,384]{1,0:T(8,128)(2,1)}, u32[]{:S(2)}, u32[]{:S(2)}) collective-permute-start(bf16[256,384]{1,0:T(8,128)(2,1)} %param.8), channel_id=1, source_target_pairs={{1,0},{2,1},{3,2},{4,3},{5,4},{6,5},{7,6},{8,7},{9,8},{10,9},{11,1... | collective-permute-start | bytes 589832 | tf_op jit(solution)/shard_map/ppermute | solution.py:16
  13.8 3.3 collective-permute-start.7
  17.1 4.0 collective-permute-start.19
  33.5 404.2 %all-reduce.1 = bf16[256,768]{1,0:T(8,128)(2,1)S(1)} all-reduce(f32[256,768]{1,0:T(8,128)S(1)} %fusion.64), channel_id=1, replica_groups=mesh['heads'=8,'tm'=64] {'tm'}, use_global_device_ids=true, to_apply=%region_1.2 | all-reduce | flops 196608 | bytes 1179648 | tf_op jit(solution)/shard_map/psum | solution.py:87
  442.4 8.1 %collective-permute-done.14 = bf16[2,2]{1,0:T(2,128)(2,1)S(1)} collective-permute-done((bf16[2,2]{1,0:T(2,128)(2,1)S(1)}, bf16[2,2]{1,0:T(2,128)(2,1)S(1)}, u32[]{:S(2)}, u32[]{:S(2)}) %collective-permute-start.14) | collective-permute-done | bytes 40 | tf_op jit(solution)/shard_map/ppermute | solution.py:16
  450.6 7.0 %collective-permute-start.8 = (bf16[2,2]{1,0:T(2,128)(2,1)S(1)}, bf16[2,2]{1,0:T(2,128)(2,1)S(1)}, u32[]{:S(2)}, u32[]{:S(2)}) collective-permute-start(bf16[2,2]{1,0:T(2,128)(2,1)S(1)} %get-tuple-element.7), channel_id=1, source_target_pairs={{2,0},{3,1},{4,2},{5,3},{6,4},{7,5},{8,6},{9,7},{10,8},{11,9},{12,... | collective-permute-start | bytes 32 | tf_op jit(solution)/shard_map/ppermute | solution.py:16
  458.9 3.9 collective-permute-start.2
  463.0 5.3 collective-permute-done.2
  468.2 6.7 collective-permute-start.15
  475.2 6.5 collective-permute-done.15
  481.6 11.3 %collective-permute-start = (bf16[256,384]{0,1:T(8,128)(2,1)S(1)}, bf16[256,384]{0,1:T(8,128)(2,1)S(1)}, u32[]{:S(2)}, u32[]{:S(2)}) collective-permute-start(bf16[256,384]{0,1:T(8,128)(2,1)S(1)} %convert_element_type.180), channel_id=1, source_target_pairs={{1,0},{2,1},{3,2},{4,3},{5,4},{6,5},{7,6},{8,7},{9,8},{10,9},{11,1... | collective-permute-start | bytes 589832 | tf_op jit(solution)/shard_map/ppermute | solution.py:16
  496.1 11.2 %collective-permute-start.6 = (bf16[256,384]{0,1:T(8,128)(2,1)S(1)}, bf16[256,384]{0,1:T(8,128)(2,1)S(1)}, u32[]{:S(2)}, u32[]{:S(2)}) collective-permute-start(bf16[256,384]{0,1:T(8,128)(2,1)S(1)} %convert_element_type.180), channel_id=1, source_target_pairs={{2,0},{3,1},{4,2},{5,3},{6,4},{7,5},{8,6},{9,7},{10,8},{11,9},{12,... | collective-permute-start | bytes 589832 | tf_op jit(solution)/shard_map/ppermute | solution.py:16
  510.4 4.0 collective-permute-start.12
  514.7 8.0 %collective-permute-done.12 = bf16[256,384]{0,1:T(8,128)(2,1)S(1)} collective-permute-done((bf16[256,384]{0,1:T(8,128)(2,1)S(1)}, bf16[256,384]{0,1:T(8,128)(2,1)S(1)}, u32[]{:S(2)}, u32[]{:S(2)}) %collective-permute-start.12) | collective-permute-done | bytes 196640 | tf_op jit(solution)/shard_map/ppermute | solution.py:16
  522.8 3.9 collective-permute-start.18
  527.0 7.3 %collective-permute-done.18 = bf16[256,384]{0,1:T(8,128)(2,1)S(1)} collective-permute-done((bf16[256,384]{0,1:T(8,128)(2,1)S(1)}, bf16[256,384]{0,1:T(8,128)(2,1)S(1)}, u32[]{:S(2)}, u32[]{:S(2)}) %collective-permute-start.18) | collective-permute-done | bytes 196640 | tf_op jit(solution)/shard_map/ppermute | solution.py:16
  537.6 5.2 collective-permute-done.21
  542.8 9.7 %collective-permute-start.9 = (bf16[256,384]{0,1:T(8,128)(2,1)S(1)}, bf16[256,384]{0,1:T(8,128)(2,1)S(1)}, u32[]{:S(2)}, u32[]{:S(2)}) collective-permute-start(bf16[256,384]{0,1:T(8,128)(2,1)S(1)} %convert_element_type.189), channel_id=1, source_target_pairs={{2,0},{3,1},{4,2},{5,3},{6,4},{7,5},{8,6},{9,7},{10,8},{11,9},{12,... | collective-permute-start | bytes 589832 | tf_op jit(solution)/shard_map/ppermute | solution.py:16
  552.9 4.9 collective-permute-done.9
  557.8 7.4 %collective-permute-start.3 = (bf16[256,384]{0,1:T(8,128)(2,1)S(1)}, bf16[256,384]{0,1:T(8,128)(2,1)S(1)}, u32[]{:S(2)}, u32[]{:S(2)}) collective-permute-start(bf16[256,384]{0,1:T(8,128)(2,1)S(1)} %convert_element_type.189), channel_id=1, source_target_pairs={{1,0},{2,1},{3,2},{4,3},{5,4},{6,5},{7,6},{8,7},{9,8},{10,9},{11,1... | collective-permute-start | bytes 589832 | tf_op jit(solution)/shard_map/ppermute | solution.py:16
  565.8 3.6 collective-permute-done.3
  569.3 15.0 %collective-permute-start.16 = (f32[256,3]{0,1:T(4,128)S(1)}, f32[256,3]{0,1:T(4,128)S(1)}, u32[]{:S(2)}, u32[]{:S(2)}) collective-permute-start(f32[256,3]{0,1:T(4,128)S(1)} %get-tuple-element.55), channel_id=1, source_target_pairs={{0,3},{1,4},{2,5},{3,6},{4,7},{5,8},{6,9},{7,10},{8,11},{9,12},{10... | collective-permute-start | bytes 9224 | tf_op jit(solution)/shard_map/ppermute | solution.py:16
  589.2 9.7 %collective-permute-start.10 = (f32[256,3]{0,1:T(4,128)S(1)}, f32[256,3]{0,1:T(4,128)S(1)}, u32[]{:S(2)}, u32[]{:S(2)}) collective-permute-start(f32[256,3]{0,1:T(4,128)S(1)} %get-tuple-element.59), channel_id=1, source_target_pairs={{0,2},{1,3},{2,4},{3,5},{4,6},{5,7},{6,8},{7,9},{8,10},{9,11},{10,... | collective-permute-start | bytes 9224 | tf_op jit(solution)/shard_map/ppermute | solution.py:16
  604.5 9.0 %collective-permute-start.22 = (f32[256,3]{0,1:T(4,128)S(1)}, f32[256,3]{0,1:T(4,128)S(1)}, u32[]{:S(2)}, u32[]{:S(2)}) collective-permute-start(f32[256,3]{0,1:T(4,128)S(1)} %get-tuple-element.53), channel_id=1, source_target_pairs={{0,4},{1,5},{2,6},{3,7},{4,8},{5,9},{6,10},{7,11},{8,12},{9,13},{1... | collective-permute-start | bytes 9224 | tf_op jit(solution)/shard_map/ppermute | solution.py:16
  615.2 15.9 %collective-permute-start.27 = (f32[256,3]{0,1:T(4,128)S(1)}, f32[256,3]{0,1:T(4,128)S(1)}, u32[]{:S(2)}, u32[]{:S(2)}) collective-permute-start(f32[256,3]{0,1:T(4,128)S(1)} %fusion.51), channel_id=1, source_target_pairs={{0,4},{1,5},{2,6},{3,7},{4,8},{5,9},{6,10},{7,11},{8,12},{9,13},{1... | collective-permute-start | bytes 9224 | tf_op jit(solution)/shard_map/ppermute | solution.py:16
  632.9 8.1 %collective-permute-start.26 = (f32[256,3]{0,1:T(4,128)S(1)}, f32[256,3]{0,1:T(4,128)S(1)}, u32[]{:S(2)}, u32[]{:S(2)}) collective-permute-start(f32[256,3]{0,1:T(4,128)S(1)} %fusion.47), channel_id=1, source_target_pairs={{0,3},{1,4},{2,5},{3,6},{4,7},{5,8},{6,9},{7,10},{8,11},{9,12},{10... | collective-permute-start | bytes 9224 | tf_op jit(solution)/shard_map/ppermute | solution.py:16
  641.0 3.5 collective-permute-start.25
  644.5 7.3 %collective-permute-start.24 = (f32[256,3]{0,1:T(4,128)S(1)}, f32[256,3]{0,1:T(4,128)S(1)}, u32[]{:S(2)}, u32[]{:S(2)}) collective-permute-start(f32[256,3]{0,1:T(4,128)S(1)} %fusion.39), channel_id=1, source_target_pairs={{0,1},{1,2},{2,3},{3,4},{4,5},{5,6},{6,7},{7,8},{8,9},{9,10},{10,1... | collective-permute-start | bytes 9224 | tf_op jit(solution)/shard_map/ppermute | solution.py:16
  651.8 11.9 %collective-permute-start.23 = (f32[256,3,128]{0,2,1:T(8,128)}, f32[256,3,128]{0,2,1:T(8,128)S(1)}, u32[]{:S(2)}, u32[]{:S(2)}) collective-permute-start(f32[256,3,128]{0,2,1:T(8,128)} %convolution_bitcast_fusion.10), channel_id=1, source_target_pairs={{0,4},{1,5},{2,6},{3,7},{4,8},{5,9},{6,10},{7,11},{8,12},{9,13},{1... | collective-permute-start | bytes 1179656 | tf_op jit(solution)/shard_map/ppermute | solution.py:16
  668.2 7.3 %collective-permute-start.5 = (f32[256,3,128]{0,2,1:T(8,128)}, f32[256,3,128]{0,2,1:T(8,128)S(1)}, u32[]{:S(2)}, u32[]{:S(2)}) collective-permute-start(f32[256,3,128]{0,2,1:T(8,128)} %convolution_bitcast_fusion.16), channel_id=1, source_target_pairs={{0,1},{1,2},{2,3},{3,4},{4,5},{5,6},{6,7},{7,8},{8,9},{9,10},{10,1... | collective-permute-start | bytes 1179656 | tf_op jit(solution)/shard_map/ppermute | solution.py:16
  679.8 7.0 %collective-permute-done.17 = f32[256,3,128]{0,2,1:T(8,128)S(1)} collective-permute-done((f32[256,3,128]{0,2,1:T(8,128)}, f32[256,3,128]{0,2,1:T(8,128)S(1)}, u32[]{:S(2)}, u32[]{:S(2)}) %collective-permute-start.17) | collective-permute-done | bytes 393248 | tf_op jit(solution)/shard_map/ppermute | solution.py:16
  686.8 11.1 %collective-permute-done.5 = f32[256,3,128]{0,2,1:T(8,128)S(1)} collective-permute-done((f32[256,3,128]{0,2,1:T(8,128)}, f32[256,3,128]{0,2,1:T(8,128)S(1)}, u32[]{:S(2)}, u32[]{:S(2)}) %collective-permute-start.5) | collective-permute-done | bytes 393248 | tf_op jit(solution)/shard_map/ppermute | solution.py:16
  (156 shorter events, 53.4 us)
Async XLA Ops:
  0.0 589.1 %collective-permute-start.1 = (bf16[256,384]{1,0:T(8,128)(2,1)}, bf16[256,384]{1,0:T(8,128)(2,1)}, u32[]{:S(2)}, u32[]{:S(2)}) collective-permute-start(bf16[256,384]{1,0:T(8,128)(2,1)} %param.8), channel_id=1, source_target_pairs={{1,0},{2,1},{3,2},{4,3},{5,4},{6,5},{7,6},{8,7},{9,8},{10,9},{11,1... | collective-permute-start | bytes 589832 | tf_op jit(solution)/shard_map/ppermute | solution.py:16
  13.8 585.1 %collective-permute-start.7 = (bf16[256,384]{1,0:T(8,128)(2,1)}, bf16[256,384]{1,0:T(8,128)(2,1)}, u32[]{:S(2)}, u32[]{:S(2)}) collective-permute-start(bf16[256,384]{1,0:T(8,128)(2,1)} %param.8), channel_id=1, source_target_pairs={{2,0},{3,1},{4,2},{5,3},{6,4},{7,5},{8,6},{9,7},{10,8},{11,9},{12,... | collective-permute-start | bytes 589832 | tf_op jit(solution)/shard_map/ppermute | solution.py:16
  17.1 587.4 %collective-permute-start.19 = (bf16[256,384]{1,0:T(8,128)(2,1)}, bf16[256,384]{1,0:T(8,128)(2,1)}, u32[]{:S(2)}, u32[]{:S(2)}) collective-permute-start(bf16[256,384]{1,0:T(8,128)(2,1)} %param.8), channel_id=1, source_target_pairs={{4,0},{5,1},{6,2},{7,3},{8,4},{9,5},{10,6},{11,7},{12,8},{13,9},{1... | collective-permute-start | bytes 589832 | tf_op jit(solution)/shard_map/ppermute | solution.py:16
  21.1 594.1 %collective-permute-start.13 = (bf16[256,384]{1,0:T(8,128)(2,1)}, bf16[256,384]{1,0:T(8,128)(2,1)}, u32[]{:S(2)}, u32[]{:S(2)}) collective-permute-start(bf16[256,384]{1,0:T(8,128)(2,1)} %param.8), channel_id=1, source_target_pairs={{3,0},{4,1},{5,2},{6,3},{7,4},{8,5},{9,6},{10,7},{11,8},{12,9},{13... | collective-permute-start | bytes 589832 | tf_op jit(solution)/shard_map/ppermute | solution.py:16
  24.0 416.4 %collective-permute-start.20 = (bf16[2,2]{1,0:T(2,128)(2,1)S(1)}, bf16[2,2]{1,0:T(2,128)(2,1)S(1)}, u32[]{:S(2)}, u32[]{:S(2)}) collective-permute-start(bf16[2,2]{1,0:T(2,128)(2,1)S(1)} %get-tuple-element.5), channel_id=1, source_target_pairs={{4,0},{5,1},{6,2},{7,3},{8,4},{9,5},{10,6},{11,7},{12,8},{13,9},{1... | collective-permute-start | bytes 32 | tf_op jit(solution)/shard_map/ppermute | solution.py:16
  440.4 10.2 %collective-permute-start.14 = (bf16[2,2]{1,0:T(2,128)(2,1)S(1)}, bf16[2,2]{1,0:T(2,128)(2,1)S(1)}, u32[]{:S(2)}, u32[]{:S(2)}) collective-permute-start(bf16[2,2]{1,0:T(2,128)(2,1)S(1)} %get-tuple-element.6), channel_id=1, source_target_pairs={{3,0},{4,1},{5,2},{6,3},{7,4},{8,5},{9,6},{10,7},{11,8},{12,9},{13... | collective-permute-start | bytes 32 | tf_op jit(solution)/shard_map/ppermute | solution.py:16
  450.6 8.3 %collective-permute-start.8 = (bf16[2,2]{1,0:T(2,128)(2,1)S(1)}, bf16[2,2]{1,0:T(2,128)(2,1)S(1)}, u32[]{:S(2)}, u32[]{:S(2)}) collective-permute-start(bf16[2,2]{1,0:T(2,128)(2,1)S(1)} %get-tuple-element.7), channel_id=1, source_target_pairs={{2,0},{3,1},{4,2},{5,3},{6,4},{7,5},{8,6},{9,7},{10,8},{11,9},{12,... | collective-permute-start | bytes 32 | tf_op jit(solution)/shard_map/ppermute | solution.py:16
  458.9 9.3 %collective-permute-start.2 = (bf16[2,2]{1,0:T(2,128)(2,1)S(1)}, bf16[2,2]{1,0:T(2,128)(2,1)S(1)}, u32[]{:S(2)}, u32[]{:S(2)}) collective-permute-start(bf16[2,2]{1,0:T(2,128)(2,1)S(1)} %get-tuple-element.8), channel_id=1, source_target_pairs={{1,0},{2,1},{3,2},{4,3},{5,4},{6,5},{7,6},{8,7},{9,8},{10,9},{11,1... | collective-permute-start | bytes 32 | tf_op jit(solution)/shard_map/ppermute | solution.py:16
  468.2 13.4 %collective-permute-start.15 = (bf16[256,384]{0,1:T(8,128)(2,1)S(1)}, bf16[256,384]{0,1:T(8,128)(2,1)S(1)}, u32[]{:S(2)}, u32[]{:S(2)}) collective-permute-start(bf16[256,384]{0,1:T(8,128)(2,1)S(1)} %convert_element_type.189), channel_id=1, source_target_pairs={{3,0},{4,1},{5,2},{6,3},{7,4},{8,5},{9,6},{10,7},{11,8},{12,9},{13... | collective-permute-start | bytes 589832 | tf_op jit(solution)/shard_map/ppermute | solution.py:16
  481.6 14.4 %collective-permute-start = (bf16[256,384]{0,1:T(8,128)(2,1)S(1)}, bf16[256,384]{0,1:T(8,128)(2,1)S(1)}, u32[]{:S(2)}, u32[]{:S(2)}) collective-permute-start(bf16[256,384]{0,1:T(8,128)(2,1)S(1)} %convert_element_type.180), channel_id=1, source_target_pairs={{1,0},{2,1},{3,2},{4,3},{5,4},{6,5},{7,6},{8,7},{9,8},{10,9},{11,1... | collective-permute-start | bytes 589832 | tf_op jit(solution)/shard_map/ppermute | solution.py:16
  496.1 14.3 %collective-permute-start.6 = (bf16[256,384]{0,1:T(8,128)(2,1)S(1)}, bf16[256,384]{0,1:T(8,128)(2,1)S(1)}, u32[]{:S(2)}, u32[]{:S(2)}) collective-permute-start(bf16[256,384]{0,1:T(8,128)(2,1)S(1)} %convert_element_type.180), channel_id=1, source_target_pairs={{2,0},{3,1},{4,2},{5,3},{6,4},{7,5},{8,6},{9,7},{10,8},{11,9},{12,... | collective-permute-start | bytes 589832 | tf_op jit(solution)/shard_map/ppermute | solution.py:16
  507.6 80.3 %copy-start.3 = (f32[256,3,256]{0,2,1:T(8,128)}, f32[256,3,256]{0,2,1:T(8,128)S(1)}, u32[]{:S(2)}) copy-start(f32[256,3,256]{0,2,1:T(8,128)S(1)} %get-tuple-element.66) | copy-start | bytes 2359300
  510.4 12.4 %collective-permute-start.12 = (bf16[256,384]{0,1:T(8,128)(2,1)S(1)}, bf16[256,384]{0,1:T(8,128)(2,1)S(1)}, u32[]{:S(2)}, u32[]{:S(2)}) collective-permute-start(bf16[256,384]{0,1:T(8,128)(2,1)S(1)} %convert_element_type.180), channel_id=1, source_target_pairs={{3,0},{4,1},{5,2},{6,3},{7,4},{8,5},{9,6},{10,7},{11,8},{12,9},{13... | collective-permute-start | bytes 589832 | tf_op jit(solution)/shard_map/ppermute | solution.py:16
  522.8 11.5 %collective-permute-start.18 = (bf16[256,384]{0,1:T(8,128)(2,1)S(1)}, bf16[256,384]{0,1:T(8,128)(2,1)S(1)}, u32[]{:S(2)}, u32[]{:S(2)}) collective-permute-start(bf16[256,384]{0,1:T(8,128)(2,1)S(1)} %convert_element_type.180), channel_id=1, source_target_pairs={{4,0},{5,1},{6,2},{7,3},{8,4},{9,5},{10,6},{11,7},{12,8},{13,9},{1... | collective-permute-start | bytes 589832 | tf_op jit(solution)/shard_map/ppermute | solution.py:16
  534.3 8.5 %collective-permute-start.21 = (bf16[256,384]{0,1:T(8,128)(2,1)S(1)}, bf16[256,384]{0,1:T(8,128)(2,1)S(1)}, u32[]{:S(2)}, u32[]{:S(2)}) collective-permute-start(bf16[256,384]{0,1:T(8,128)(2,1)S(1)} %convert_element_type.189), channel_id=1, source_target_pairs={{4,0},{5,1},{6,2},{7,3},{8,4},{9,5},{10,6},{11,7},{12,8},{13,9},{1... | collective-permute-start | bytes 589832 | tf_op jit(solution)/shard_map/ppermute | solution.py:16
  537.6 50.6 %copy-start = (f32[256,3,256]{0,2,1:T(8,128)}, f32[256,3,256]{0,2,1:T(8,128)S(1)}, u32[]{:S(2)}) copy-start(f32[256,3,256]{0,2,1:T(8,128)S(1)} %get-tuple-element.52) | copy-start | bytes 2359300
  542.8 15.0 %collective-permute-start.9 = (bf16[256,384]{0,1:T(8,128)(2,1)S(1)}, bf16[256,384]{0,1:T(8,128)(2,1)S(1)}, u32[]{:S(2)}, u32[]{:S(2)}) collective-permute-start(bf16[256,384]{0,1:T(8,128)(2,1)S(1)} %convert_element_type.189), channel_id=1, source_target_pairs={{2,0},{3,1},{4,2},{5,3},{6,4},{7,5},{8,6},{9,7},{10,8},{11,9},{12,... | collective-permute-start | bytes 589832 | tf_op jit(solution)/shard_map/ppermute | solution.py:16
  557.8 11.5 %collective-permute-start.3 = (bf16[256,384]{0,1:T(8,128)(2,1)S(1)}, bf16[256,384]{0,1:T(8,128)(2,1)S(1)}, u32[]{:S(2)}, u32[]{:S(2)}) collective-permute-start(bf16[256,384]{0,1:T(8,128)(2,1)S(1)} %convert_element_type.189), channel_id=1, source_target_pairs={{1,0},{2,1},{3,2},{4,3},{5,4},{6,5},{7,6},{8,7},{9,8},{10,9},{11,1... | collective-permute-start | bytes 589832 | tf_op jit(solution)/shard_map/ppermute | solution.py:16
  569.3 63.5 %collective-permute-start.16 = (f32[256,3]{0,1:T(4,128)S(1)}, f32[256,3]{0,1:T(4,128)S(1)}, u32[]{:S(2)}, u32[]{:S(2)}) collective-permute-start(f32[256,3]{0,1:T(4,128)S(1)} %get-tuple-element.55), channel_id=1, source_target_pairs={{0,3},{1,4},{2,5},{3,6},{4,7},{5,8},{6,9},{7,10},{8,11},{9,12},{10... | collective-permute-start | bytes 9224 | tf_op jit(solution)/shard_map/ppermute | solution.py:16
  589.2 51.8 %collective-permute-start.10 = (f32[256,3]{0,1:T(4,128)S(1)}, f32[256,3]{0,1:T(4,128)S(1)}, u32[]{:S(2)}, u32[]{:S(2)}) collective-permute-start(f32[256,3]{0,1:T(4,128)S(1)} %get-tuple-element.59), channel_id=1, source_target_pairs={{0,2},{1,3},{2,4},{3,5},{4,6},{5,7},{6,8},{7,9},{8,10},{9,11},{10,... | collective-permute-start | bytes 9224 | tf_op jit(solution)/shard_map/ppermute | solution.py:16
  598.9 45.6 %collective-permute-start.4 = (f32[256,3]{0,1:T(4,128)S(1)}, f32[256,3]{0,1:T(4,128)S(1)}, u32[]{:S(2)}, u32[]{:S(2)}) collective-permute-start(f32[256,3]{0,1:T(4,128)S(1)} %get-tuple-element.63), channel_id=1, source_target_pairs={{0,1},{1,2},{2,3},{3,4},{4,5},{5,6},{6,7},{7,8},{8,9},{9,10},{10,1... | collective-permute-start | bytes 9224 | tf_op jit(solution)/shard_map/ppermute | solution.py:16
  604.5 59.3 %collective-permute-start.22 = (f32[256,3]{0,1:T(4,128)S(1)}, f32[256,3]{0,1:T(4,128)S(1)}, u32[]{:S(2)}, u32[]{:S(2)}) collective-permute-start(f32[256,3]{0,1:T(4,128)S(1)} %get-tuple-element.53), channel_id=1, source_target_pairs={{0,4},{1,5},{2,6},{3,7},{4,8},{5,9},{6,10},{7,11},{8,12},{9,13},{1... | collective-permute-start | bytes 9224 | tf_op jit(solution)/shard_map/ppermute | solution.py:16
  615.2 36.7 %collective-permute-start.27 = (f32[256,3]{0,1:T(4,128)S(1)}, f32[256,3]{0,1:T(4,128)S(1)}, u32[]{:S(2)}, u32[]{:S(2)}) collective-permute-start(f32[256,3]{0,1:T(4,128)S(1)} %fusion.51), channel_id=1, source_target_pairs={{0,4},{1,5},{2,6},{3,7},{4,8},{5,9},{6,10},{7,11},{8,12},{9,13},{1... | collective-permute-start | bytes 9224 | tf_op jit(solution)/shard_map/ppermute | solution.py:16
  632.8 42.7 %copy-start.8 = (bf16[256,384]{0,1:T(8,128)(2,1)S(1)}, bf16[256,384]{0,1:T(8,128)(2,1)}, u32[]{:S(2)}) copy-start(bf16[256,384]{0,1:T(8,128)(2,1)} %copy.94) | copy-start | bytes 589828
  632.9 32.9 %collective-permute-start.26 = (f32[256,3]{0,1:T(4,128)S(1)}, f32[256,3]{0,1:T(4,128)S(1)}, u32[]{:S(2)}, u32[]{:S(2)}) collective-permute-start(f32[256,3]{0,1:T(4,128)S(1)} %fusion.47), channel_id=1, source_target_pairs={{0,3},{1,4},{2,5},{3,6},{4,7},{5,8},{6,9},{7,10},{8,11},{9,12},{10... | collective-permute-start | bytes 9224 | tf_op jit(solution)/shard_map/ppermute | solution.py:16
  641.0 27.2 %collective-permute-start.25 = (f32[256,3]{0,1:T(4,128)S(1)}, f32[256,3]{0,1:T(4,128)S(1)}, u32[]{:S(2)}, u32[]{:S(2)}) collective-permute-start(f32[256,3]{0,1:T(4,128)S(1)} %fusion.43), channel_id=1, source_target_pairs={{0,2},{1,3},{2,4},{3,5},{4,6},{5,7},{6,8},{7,9},{8,10},{9,11},{10,... | collective-permute-start | bytes 9224 | tf_op jit(solution)/shard_map/ppermute | solution.py:16
  644.5 31.0 %collective-permute-start.24 = (f32[256,3]{0,1:T(4,128)S(1)}, f32[256,3]{0,1:T(4,128)S(1)}, u32[]{:S(2)}, u32[]{:S(2)}) collective-permute-start(f32[256,3]{0,1:T(4,128)S(1)} %fusion.39), channel_id=1, source_target_pairs={{0,1},{1,2},{2,3},{3,4},{4,5},{5,6},{6,7},{7,8},{8,9},{9,10},{10,1... | collective-permute-start | bytes 9224 | tf_op jit(solution)/shard_map/ppermute | solution.py:16
  651.8 27.9 %collective-permute-start.23 = (f32[256,3,128]{0,2,1:T(8,128)}, f32[256,3,128]{0,2,1:T(8,128)S(1)}, u32[]{:S(2)}, u32[]{:S(2)}) collective-permute-start(f32[256,3,128]{0,2,1:T(8,128)} %convolution_bitcast_fusion.10), channel_id=1, source_target_pairs={{0,4},{1,5},{2,6},{3,7},{4,8},{5,9},{6,10},{7,11},{8,12},{9,13},{1... | collective-permute-start | bytes 1179656 | tf_op jit(solution)/shard_map/ppermute | solution.py:16
  663.8 23.0 %collective-permute-start.17 = (f32[256,3,128]{0,2,1:T(8,128)}, f32[256,3,128]{0,2,1:T(8,128)S(1)}, u32[]{:S(2)}, u32[]{:S(2)}) collective-permute-start(f32[256,3,128]{0,2,1:T(8,128)} %convolution_bitcast_fusion.12), channel_id=1, source_target_pairs={{0,3},{1,4},{2,5},{3,6},{4,7},{5,8},{6,9},{7,10},{8,11},{9,12},{10... | collective-permute-start | bytes 1179656 | tf_op jit(solution)/shard_map/ppermute | solution.py:16
  665.7 21.1 %collective-permute-start.11 = (f32[256,3,128]{0,2,1:T(8,128)}, f32[256,3,128]{0,2,1:T(8,128)S(1)}, u32[]{:S(2)}, u32[]{:S(2)}) collective-permute-start(f32[256,3,128]{0,2,1:T(8,128)} %convolution_bitcast_fusion.14), channel_id=1, source_target_pairs={{0,2},{1,3},{2,4},{3,5},{4,6},{5,7},{6,8},{7,9},{8,10},{9,11},{10,... | collective-permute-start | bytes 1179656 | tf_op jit(solution)/shard_map/ppermute | solution.py:16
  668.2 29.7 %collective-permute-start.5 = (f32[256,3,128]{0,2,1:T(8,128)}, f32[256,3,128]{0,2,1:T(8,128)S(1)}, u32[]{:S(2)}, u32[]{:S(2)}) collective-permute-start(f32[256,3,128]{0,2,1:T(8,128)} %convolution_bitcast_fusion.16), channel_id=1, source_target_pairs={{0,1},{1,2},{2,3},{3,4},{4,5},{5,6},{6,7},{7,8},{8,9},{9,10},{10,1... | collective-permute-start | bytes 1179656 | tf_op jit(solution)/shard_map/ppermute | solution.py:16
  679.5 18.4 %copy-start.4 = (f32[256,3,256]{0,2,1:T(8,128)S(1)}, f32[256,3,256]{0,2,1:T(8,128)}, u32[]{:S(2)}) copy-start(f32[256,3,256]{0,2,1:T(8,128)} %copy-done.3) | copy-start | bytes 2359300
  (11 other events, 28.7 us)
where the time goes:
time: 700 us; the launch traced here: 699 us
  blocking collectives  404 us (58%)
  starting transfers between devices  189 us (27%)
  waiting for transfers between devices  72.8 us (10%)
  local copies, waits for them, and re-layouts  16.8 us (2%)
  matrix products  10.8 us (2%)
    psum x1, blocking collectives, on_device(): sink_table = lax.psum(sink_table, 'tm').astype(jnp.bfloat16)  404 us
    ppermute x28, starting transfers between devices, shifted(): return lax.ppermute(shard, axis, pairs)  189 us
    ppermute x28, waiting for transfers between devices, shifted(): return lax.ppermute(shard, axis, pairs)  72.8 us
  transfers between devices with their start and end apart: 28, of which 13 were waited for; matrix products, arithmetic and copies ran while one was open for 4% of the time, Pallas kernels for 0%

commit v1 on v0

--- a/solution.py
+++ b/solution.py
@@ -84,7 +84,7 @@
     sink_table = jnp.dot(
         one_hot, jnp.concatenate([k_rot, values], axis=1), preferred_element_type=jnp.float32
     )
-    sink_table = lax.psum(sink_table, "tm").astype(jnp.bfloat16)
+    sink_table = jnp.sum(lax.all_gather(sink_table, "tm"), axis=0).astype(jnp.bfloat16)
     sink_keys = sink_table[:, :feature_width].reshape(SINK, HG, HD)
     sink_values = sink_table[:, feature_width:].reshape(SINK, HG, HD)
     sink_keep = jnp.ones((tiles, SINK // TILE), jnp.float32)

time: 700 us -> 880 us (1.26)
  the two profiles are of different devices: /device:TPU:4 before, /device:TPU:266 now
where the time goes in v1:
time: 880 us; the launch traced here: 878 us
  waiting for transfers between devices  627 us (71%)
  starting transfers between devices  153 us (17%)
  other arithmetic  34.8 us (4%)
  matrix products  29.5 us (3%)
  local copies, waits for them, and re-layouts  20 us (2%)
  between operations  14.2 us (2%)
    all_gather x1, waiting for transfers between devices, on_device(): lax.all_gather(sink_table, 'tm')  586 us
    ppermute x28, starting transfers between devices, shifted(): return lax.ppermute(shard, axis, pairs)  153 us
    ppermute x28, waiting for transfers between devices, shifted(): return lax.ppermute(shard, axis, pairs)  40.5 us
    reduce_sum x1, other arithmetic, on_device(): jnp.sum(lax.all_gather(sink_table, 'tm'), axis=0).astype(jnp.bfloat16)  18.3 us
  transfers between devices with their start and end apart: 29, of which 9 were waited for; matrix products, arithmetic and copies ran while one was open for 8% of the time, Pallas kernels for 0%

profile of v1, /device:TPU:266, one launch (start us, length us, event | category | flops | bytes accessed | tf_op | source)
XLA Modules:
  0.0 878.5 jit_solution(8296033587206363455)
XLA Ops:
  15.1 2.4 collective-permute-start.6
  17.4 11.5 %collective-permute-start = (bf16[256,384]{0,1:T(8,128)(2,1)S(1)}, bf16[256,384]{0,1:T(8,128)(2,1)}, u32[]{:S(2)}, u32[]{:S(2)}) collective-permute-start(bf16[256,384]{0,1:T(8,128)(2,1)S(1)} %convert_element_type.180), channel_id=1, source_target_pairs={{1,0},{2,1},{3,2},{4,3},{5,4},{6,5},{7,6},{8,7},{9,8},{10,9},{11,1... | collective-permute-start | bytes 589832 | tf_op jit(solution)/shard_map/ppermute | solution.py:16
  31.8 3.3 collective-permute-start.9
  36.0 3.2 collective-permute-start.8
  42.6 11.3 %collective-permute-start.14 = (bf16[2,2]{1,0:T(2,128)(2,1)S(1)}, bf16[2,2]{1,0:T(2,128)(2,1)S(1)}, u32[]{:S(2)}, u32[]{:S(2)}) collective-permute-start(bf16[2,2]{1,0:T(2,128)(2,1)S(1)} %get-tuple-element.6), channel_id=1, source_target_pairs={{3,0},{4,1},{5,2},{6,3},{7,4},{8,5},{9,6},{10,7},{11,8},{12,9},{13... | collective-permute-start | bytes 32 | tf_op jit(solution)/shard_map/ppermute | solution.py:16
  55.2 7.0 collective-permute-start.2
  62.4 3.0 collective-permute-done.2
  65.4 10.2 %collective-permute-start.20 = (bf16[2,2]{1,0:T(2,128)(2,1)S(1)}, bf16[2,2]{1,0:T(2,128)(2,1)S(1)}, u32[]{:S(2)}, u32[]{:S(2)}) collective-permute-start(bf16[2,2]{1,0:T(2,128)(2,1)S(1)} %get-tuple-element.5), channel_id=1, source_target_pairs={{4,0},{5,1},{6,2},{7,3},{8,4},{9,5},{10,6},{11,7},{12,8},{13,9},{1... | collective-permute-start | bytes 32 | tf_op jit(solution)/shard_map/ppermute | solution.py:16
  76.8 3.3 collective-permute-start.15
  80.4 11.1 %collective-permute-start.3 = (bf16[256,384]{0,1:T(8,128)(2,1)}, bf16[256,384]{0,1:T(8,128)(2,1)S(1)}, u32[]{:S(2)}, u32[]{:S(2)}) collective-permute-start(bf16[256,384]{0,1:T(8,128)(2,1)} %convert_element_type.189), channel_id=1, source_target_pairs={{1,0},{2,1},{3,2},{4,3},{5,4},{6,5},{7,6},{8,7},{9,8},{10,9},{11,1... | collective-permute-start | bytes 589832 | tf_op jit(solution)/shard_map/ppermute | solution.py:16
  98.8 4.9 collective-permute-start.13
  105.6 3.4 collective-permute-done.3
  109.0 6.7 collective-permute-start.19
  118.0 6.8 collective-permute-start.1
  130.3 6.4 collective-permute-start.18
  142.1 7.1 collective-permute-start.16
  150.1 3.9 collective-permute-start.4
  157.7 4.1 collective-permute-start.22
  164.2 6.8 collective-permute-start.24
  174.7 2.2 convolution_bitcast_fusion.14
  183.5 586.3 %all-gather.3.cloned.1.call-done = f32[16384,768]{1,0:T(8,128)} async-done(((f32[256,768]{1,0:T(8,128)}), f32[16384,768]{1,0:T(8,128)}) %all-gather.3.cloned.1.call-update) | async-done | bytes 50331664 | tf_op jit(solution)/shard_map/all_gather | solution.py:87
  769.8 18.3 %reduce_sum.99 = bf16[256,768]{1,0:T(8,128)(2,1)} reduce(f32[64,256,768]{2,1,0:T(8,128)} %bitcast.244, f32[]{:T(128)} %constant.13.clone.1), dimensions={0}, to_apply=%region_1.2 | reduce | flops 12386304 | bytes 50724868 | tf_op jit(solution)/shard_map/reduce_sum | solution.py:87
  793.0 3.4 collective-permute-start.25
  796.4 9.1 %collective-permute-start.26 = (f32[256,3]{0,1:T(4,128)}, f32[256,3]{0,1:T(4,128)}, u32[]{:S(2)}, u32[]{:S(2)}) collective-permute-start(f32[256,3]{0,1:T(4,128)} %fusion.47), channel_id=1, source_target_pairs={{0,3},{1,4},{2,5},{3,6},{4,7},{5,8},{6,9},{7,10},{8,11},{9,12},{10... | collective-permute-start | bytes 9224 | tf_op jit(solution)/shard_map/ppermute | solution.py:16
  805.4 3.5 collective-permute-start.27
  812.2 2.5 collective-permute-start.11
  814.7 5.0 collective-permute-start.17
  819.7 6.5 collective-permute-start.5
  826.3 5.5 collective-permute-start.23
  838.3 3.1 collective-permute-done.17
  841.4 11.6 %collective-permute-done.5 = f32[256,3,128]{0,2,1:T(8,128)S(1)} collective-permute-done((f32[256,3,128]{0,2,1:T(8,128)}, f32[256,3,128]{0,2,1:T(8,128)S(1)}, u32[]{:S(2)}, u32[]{:S(2)}) %collective-permute-start.5) | collective-permute-done | bytes 393248 | tf_op jit(solution)/shard_map/ppermute | solution.py:16
  853.1 15.9 %collective-permute-done.23 = f32[256,3,128]{0,2,1:T(8,128)S(1)} collective-permute-done((f32[256,3,128]{0,2,1:T(8,128)}, f32[256,3,128]{0,2,1:T(8,128)S(1)}, u32[]{:S(2)}, u32[]{:S(2)}) %collective-permute-start.23) | collective-permute-done | bytes 393248 | tf_op jit(solution)/shard_map/ppermute | solution.py:16
  (165 shorter events, 74.8 us)
Async XLA Ops:
  6.5 763.3 %all-gather.3.cloned.1.call-start = ((), (), s32[]{:S(2)}) async-start(), calls=%async_computation | async-start | bytes 51118080 | tf_op jit(solution)/shard_map/all_gather | solution.py:87
  13.1 67.2 %collective-permute-start.12 = (bf16[256,384]{0,1:T(8,128)(2,1)S(1)}, bf16[256,384]{0,1:T(8,128)(2,1)S(1)}, u32[]{:S(2)}, u32[]{:S(2)}) collective-permute-start(bf16[256,384]{0,1:T(8,128)(2,1)S(1)} %convert_element_type.180), channel_id=1, source_target_pairs={{3,0},{4,1},{5,2},{6,3},{7,4},{8,5},{9,6},{10,7},{11,8},{12,9},{13... | collective-permute-start | bytes 589832 | tf_op jit(solution)/shard_map/ppermute | solution.py:16
  15.1 76.8 %collective-permute-start.6 = (bf16[256,384]{0,1:T(8,128)(2,1)S(1)}, bf16[256,384]{0,1:T(8,128)(2,1)S(1)}, u32[]{:S(2)}, u32[]{:S(2)}) collective-permute-start(bf16[256,384]{0,1:T(8,128)(2,1)S(1)} %convert_element_type.180), channel_id=1, source_target_pairs={{2,0},{3,1},{4,2},{5,3},{6,4},{7,5},{8,6},{9,7},{10,8},{11,9},{12,... | collective-permute-start | bytes 589832 | tf_op jit(solution)/shard_map/ppermute | solution.py:16
  17.4 140.3 %collective-permute-start = (bf16[256,384]{0,1:T(8,128)(2,1)S(1)}, bf16[256,384]{0,1:T(8,128)(2,1)}, u32[]{:S(2)}, u32[]{:S(2)}) collective-permute-start(bf16[256,384]{0,1:T(8,128)(2,1)S(1)} %convert_element_type.180), channel_id=1, source_target_pairs={{1,0},{2,1},{3,2},{4,3},{5,4},{6,5},{7,6},{8,7},{9,8},{10,9},{11,1... | collective-permute-start | bytes 589832 | tf_op jit(solution)/shard_map/ppermute | solution.py:16
  31.8 63.2 %collective-permute-start.9 = (bf16[256,384]{0,1:T(8,128)(2,1)}, bf16[256,384]{0,1:T(8,128)(2,1)}, u32[]{:S(2)}, u32[]{:S(2)}) collective-permute-start(bf16[256,384]{0,1:T(8,128)(2,1)} %convert_element_type.189), channel_id=1, source_target_pairs={{2,0},{3,1},{4,2},{5,3},{6,4},{7,5},{8,6},{9,7},{10,8},{11,9},{12,... | collective-permute-start | bytes 589832 | tf_op jit(solution)/shard_map/ppermute | solution.py:16
  36.0 6.5 collective-permute-start.8
  40.4 130.6 %copy-start.17 = (f32[1,2,2,128]{3,1,2,0:T(2,128)}, f32[1,2,2,128]{3,1,2,0:T(2,128)S(1)}, u32[]{:S(2)}) copy-start(f32[1,2,2,128]{3,1,2,0:T(2,128)S(1)} %copy.215) | copy-start | bytes 6148
  42.6 12.6 %collective-permute-start.14 = (bf16[2,2]{1,0:T(2,128)(2,1)S(1)}, bf16[2,2]{1,0:T(2,128)(2,1)S(1)}, u32[]{:S(2)}, u32[]{:S(2)}) collective-permute-start(bf16[2,2]{1,0:T(2,128)(2,1)S(1)} %get-tuple-element.6), channel_id=1, source_target_pairs={{3,0},{4,1},{5,2},{6,3},{7,4},{8,5},{9,6},{10,7},{11,8},{12,9},{13... | collective-permute-start | bytes 32 | tf_op jit(solution)/shard_map/ppermute | solution.py:16
  55.2 10.2 %collective-permute-start.2 = (bf16[2,2]{1,0:T(2,128)(2,1)S(1)}, bf16[2,2]{1,0:T(2,128)(2,1)S(1)}, u32[]{:S(2)}, u32[]{:S(2)}) collective-permute-start(bf16[2,2]{1,0:T(2,128)(2,1)S(1)} %get-tuple-element.8), channel_id=1, source_target_pairs={{1,0},{2,1},{3,2},{4,3},{5,4},{6,5},{7,6},{8,7},{9,8},{10,9},{11,1... | collective-permute-start | bytes 32 | tf_op jit(solution)/shard_map/ppermute | solution.py:16
  65.4 11.4 %collective-permute-start.20 = (bf16[2,2]{1,0:T(2,128)(2,1)S(1)}, bf16[2,2]{1,0:T(2,128)(2,1)S(1)}, u32[]{:S(2)}, u32[]{:S(2)}) collective-permute-start(bf16[2,2]{1,0:T(2,128)(2,1)S(1)} %get-tuple-element.5), channel_id=1, source_target_pairs={{4,0},{5,1},{6,2},{7,3},{8,4},{9,5},{10,6},{11,7},{12,8},{13,9},{1... | collective-permute-start | bytes 32 | tf_op jit(solution)/shard_map/ppermute | solution.py:16
  76.8 22.0 %collective-permute-start.15 = (bf16[256,384]{0,1:T(8,128)(2,1)}, bf16[256,384]{0,1:T(8,128)(2,1)}, u32[]{:S(2)}, u32[]{:S(2)}) collective-permute-start(bf16[256,384]{0,1:T(8,128)(2,1)} %convert_element_type.189), channel_id=1, source_target_pairs={{3,0},{4,1},{5,2},{6,3},{7,4},{8,5},{9,6},{10,7},{11,8},{12,9},{13... | collective-permute-start | bytes 589832 | tf_op jit(solution)/shard_map/ppermute | solution.py:16
  80.4 28.6 %collective-permute-start.3 = (bf16[256,384]{0,1:T(8,128)(2,1)}, bf16[256,384]{0,1:T(8,128)(2,1)S(1)}, u32[]{:S(2)}, u32[]{:S(2)}) collective-permute-start(bf16[256,384]{0,1:T(8,128)(2,1)} %convert_element_type.189), channel_id=1, source_target_pairs={{1,0},{2,1},{3,2},{4,3},{5,4},{6,5},{7,6},{8,7},{9,8},{10,9},{11,1... | collective-permute-start | bytes 589832 | tf_op jit(solution)/shard_map/ppermute | solution.py:16
  91.8 26.2 %collective-permute-start.21 = (bf16[256,384]{0,1:T(8,128)(2,1)}, bf16[256,384]{0,1:T(8,128)(2,1)S(1)}, u32[]{:S(2)}, u32[]{:S(2)}) collective-permute-start(bf16[256,384]{0,1:T(8,128)(2,1)} %convert_element_type.189), channel_id=1, source_target_pairs={{4,0},{5,1},{6,2},{7,3},{8,4},{9,5},{10,6},{11,7},{12,8},{13,9},{1... | collective-permute-start | bytes 589832 | tf_op jit(solution)/shard_map/ppermute | solution.py:16
  95.0 34.6 %collective-permute-start.7 = (bf16[256,384]{1,0:T(8,128)(2,1)}, bf16[256,384]{1,0:T(8,128)(2,1)S(1)}, u32[]{:S(2)}, u32[]{:S(2)}) collective-permute-start(bf16[256,384]{1,0:T(8,128)(2,1)} %param.8), channel_id=1, source_target_pairs={{2,0},{3,1},{4,2},{5,3},{6,4},{7,5},{8,6},{9,7},{10,8},{11,9},{12,... | collective-permute-start | bytes 589832 | tf_op jit(solution)/shard_map/ppermute | solution.py:16
  98.8 27.8 %copy-start = (f32[256,3,256]{0,2,1:T(8,128)}, f32[256,3,256]{0,2,1:T(8,128)S(1)}, u32[]{:S(2)}) copy-start(f32[256,3,256]{0,2,1:T(8,128)S(1)} %get-tuple-element.60) | copy-start | bytes 2359300
  98.8 39.6 %collective-permute-start.13 = (bf16[256,384]{1,0:T(8,128)(2,1)}, bf16[256,384]{1,0:T(8,128)(2,1)}, u32[]{:S(2)}, u32[]{:S(2)}) collective-permute-start(bf16[256,384]{1,0:T(8,128)(2,1)} %param.8), channel_id=1, source_target_pairs={{3,0},{4,1},{5,2},{6,3},{7,4},{8,5},{9,6},{10,7},{11,8},{12,9},{13... | collective-permute-start | bytes 589832 | tf_op jit(solution)/shard_map/ppermute | solution.py:16
  105.6 22.6 %copy-start.1 = (f32[256,3,256]{0,2,1:T(8,128)}, f32[256,3,256]{0,2,1:T(8,128)S(1)}, u32[]{:S(2)}) copy-start(f32[256,3,256]{0,2,1:T(8,128)S(1)} %get-tuple-element.56) | copy-start | bytes 2359300
  109.0 33.1 %collective-permute-start.19 = (bf16[256,384]{1,0:T(8,128)(2,1)}, bf16[256,384]{1,0:T(8,128)(2,1)S(1)}, u32[]{:S(2)}, u32[]{:S(2)}) collective-permute-start(bf16[256,384]{1,0:T(8,128)(2,1)} %param.8), channel_id=1, source_target_pairs={{4,0},{5,1},{6,2},{7,3},{8,4},{9,5},{10,6},{11,7},{12,8},{13,9},{1... | collective-permute-start | bytes 589832 | tf_op jit(solution)/shard_map/ppermute | solution.py:16
  118.0 32.1 %collective-permute-start.1 = (bf16[256,384]{1,0:T(8,128)(2,1)}, bf16[256,384]{1,0:T(8,128)(2,1)}, u32[]{:S(2)}, u32[]{:S(2)}) collective-permute-start(bf16[256,384]{1,0:T(8,128)(2,1)} %param.8), channel_id=1, source_target_pairs={{1,0},{2,1},{3,2},{4,3},{5,4},{6,5},{7,6},{8,7},{9,8},{10,9},{11,1... | collective-permute-start | bytes 589832 | tf_op jit(solution)/shard_map/ppermute | solution.py:16
  130.3 33.9 %collective-permute-start.18 = (bf16[256,384]{0,1:T(8,128)(2,1)S(1)}, bf16[256,384]{0,1:T(8,128)(2,1)S(1)}, u32[]{:S(2)}, u32[]{:S(2)}) collective-permute-start(bf16[256,384]{0,1:T(8,128)(2,1)S(1)} %convert_element_type.180), channel_id=1, source_target_pairs={{4,0},{5,1},{6,2},{7,3},{8,4},{9,5},{10,6},{11,7},{12,8},{13,9},{1... | collective-permute-start | bytes 589832 | tf_op jit(solution)/shard_map/ppermute | solution.py:16
  138.5 654.5 %collective-permute-start.10 = (f32[256,3]{0,1:T(4,128)}, f32[256,3]{0,1:T(4,128)}, u32[]{:S(2)}, u32[]{:S(2)}) collective-permute-start(f32[256,3]{0,1:T(4,128)} %get-tuple-element.59), channel_id=1, source_target_pairs={{0,2},{1,3},{2,4},{3,5},{4,6},{5,7},{6,8},{7,9},{8,10},{9,11},{10,... | collective-permute-start | bytes 9224 | tf_op jit(solution)/shard_map/ppermute | solution.py:16
  142.1 654.2 %collective-permute-start.16 = (f32[256,3]{0,1:T(4,128)}, f32[256,3]{0,1:T(4,128)}, u32[]{:S(2)}, u32[]{:S(2)}) collective-permute-start(f32[256,3]{0,1:T(4,128)} %get-tuple-element.55), channel_id=1, source_target_pairs={{0,3},{1,4},{2,5},{3,6},{4,7},{5,8},{6,9},{7,10},{8,11},{9,12},{10... | collective-permute-start | bytes 9224 | tf_op jit(solution)/shard_map/ppermute | solution.py:16
  150.1 655.3 %collective-permute-start.4 = (f32[256,3]{0,1:T(4,128)}, f32[256,3]{0,1:T(4,128)}, u32[]{:S(2)}, u32[]{:S(2)}) collective-permute-start(f32[256,3]{0,1:T(4,128)} %get-tuple-element.63), channel_id=1, source_target_pairs={{0,1},{1,2},{2,3},{3,4},{4,5},{5,6},{6,7},{7,8},{8,9},{9,10},{10,1... | collective-permute-start | bytes 9224 | tf_op jit(solution)/shard_map/ppermute | solution.py:16
  157.7 674.1 %collective-permute-start.22 = (f32[256,3]{0,1:T(4,128)}, f32[256,3]{0,1:T(4,128)}, u32[]{:S(2)}, u32[]{:S(2)}) collective-permute-start(f32[256,3]{0,1:T(4,128)} %get-tuple-element.53), channel_id=1, source_target_pairs={{0,4},{1,5},{2,6},{3,7},{4,8},{5,9},{6,10},{7,11},{8,12},{9,13},{1... | collective-permute-start | bytes 9224 | tf_op jit(solution)/shard_map/ppermute | solution.py:16
  164.2 648.0 %collective-permute-start.24 = (f32[256,3]{0,1:T(4,128)}, f32[256,3]{0,1:T(4,128)}, u32[]{:S(2)}, u32[]{:S(2)}) collective-permute-start(f32[256,3]{0,1:T(4,128)} %fusion.39), channel_id=1, source_target_pairs={{0,1},{1,2},{2,3},{3,4},{4,5},{5,6},{6,7},{7,8},{8,9},{9,10},{10,1... | collective-permute-start | bytes 9224 | tf_op jit(solution)/shard_map/ppermute | solution.py:16
  793.0 21.7 %collective-permute-start.25 = (f32[256,3]{0,1:T(4,128)}, f32[256,3]{0,1:T(4,128)}, u32[]{:S(2)}, u32[]{:S(2)}) collective-permute-start(f32[256,3]{0,1:T(4,128)} %fusion.43), channel_id=1, source_target_pairs={{0,2},{1,3},{2,4},{3,5},{4,6},{5,7},{6,8},{7,9},{8,10},{9,11},{10,... | collective-permute-start | bytes 9224 | tf_op jit(solution)/shard_map/ppermute | solution.py:16
  796.4 23.3 %collective-permute-start.26 = (f32[256,3]{0,1:T(4,128)}, f32[256,3]{0,1:T(4,128)}, u32[]{:S(2)}, u32[]{:S(2)}) collective-permute-start(f32[256,3]{0,1:T(4,128)} %fusion.47), channel_id=1, source_target_pairs={{0,3},{1,4},{2,5},{3,6},{4,7},{5,8},{6,9},{7,10},{8,11},{9,12},{10... | collective-permute-start | bytes 9224 | tf_op jit(solution)/shard_map/ppermute | solution.py:16
  805.4 20.8 %collective-permute-start.27 = (f32[256,3]{0,1:T(4,128)}, f32[256,3]{0,1:T(4,128)}, u32[]{:S(2)}, u32[]{:S(2)}) collective-permute-start(f32[256,3]{0,1:T(4,128)} %fusion.51), channel_id=1, source_target_pairs={{0,4},{1,5},{2,6},{3,7},{4,8},{5,9},{6,10},{7,11},{8,12},{9,13},{1... | collective-permute-start | bytes 9224 | tf_op jit(solution)/shard_map/ppermute | solution.py:16
  812.2 26.1 %collective-permute-start.11 = (f32[256,3,128]{0,2,1:T(8,128)}, f32[256,3,128]{0,2,1:T(8,128)S(1)}, u32[]{:S(2)}, u32[]{:S(2)}) collective-permute-start(f32[256,3,128]{0,2,1:T(8,128)} %convolution_bitcast_fusion.14), channel_id=1, source_target_pairs={{0,2},{1,3},{2,4},{3,5},{4,6},{5,7},{6,8},{7,9},{8,10},{9,11},{10,... | collective-permute-start | bytes 1179656 | tf_op jit(solution)/shard_map/ppermute | solution.py:16
  814.7 26.7 %collective-permute-start.17 = (f32[256,3,128]{0,2,1:T(8,128)}, f32[256,3,128]{0,2,1:T(8,128)S(1)}, u32[]{:S(2)}, u32[]{:S(2)}) collective-permute-start(f32[256,3,128]{0,2,1:T(8,128)} %convolution_bitcast_fusion.12), channel_id=1, source_target_pairs={{0,3},{1,4},{2,5},{3,6},{4,7},{5,8},{6,9},{7,10},{8,11},{9,12},{10... | collective-permute-start | bytes 1179656 | tf_op jit(solution)/shard_map/ppermute | solution.py:16
  819.7 33.4 %collective-permute-start.5 = (f32[256,3,128]{0,2,1:T(8,128)}, f32[256,3,128]{0,2,1:T(8,128)S(1)}, u32[]{:S(2)}, u32[]{:S(2)}) collective-permute-start(f32[256,3,128]{0,2,1:T(8,128)} %convolution_bitcast_fusion.16), channel_id=1, source_target_pairs={{0,1},{1,2},{2,3},{3,4},{4,5},{5,6},{6,7},{7,8},{8,9},{9,10},{10,1... | collective-permute-start | bytes 1179656 | tf_op jit(solution)/shard_map/ppermute | solution.py:16
  826.3 42.7 %collective-permute-start.23 = (f32[256,3,128]{0,2,1:T(8,128)}, f32[256,3,128]{0,2,1:T(8,128)S(1)}, u32[]{:S(2)}, u32[]{:S(2)}) collective-permute-start(f32[256,3,128]{0,2,1:T(8,128)} %convolution_bitcast_fusion.10), channel_id=1, source_target_pairs={{0,4},{1,5},{2,6},{3,7},{4,8},{5,9},{6,10},{7,11},{8,12},{9,13},{1... | collective-permute-start | bytes 1179656 | tf_op jit(solution)/shard_map/ppermute | solution.py:16
  (15 other events, 95.4 us)
Sparse Core Ops, SparseCore 0:
  13.3 756.5 all-gather.2
